TPU v7x, 32 devices: a whole 2x2x4 slice. The times are simulated.
32 devices in a mesh: lon: 8 (over z, x), lat: 4 (over y, core).
Axes of the slice: x: 2, y: 2, z: 4, core: 2. Of those that a mesh axis runs over, the one named last changes fastest.
Arguments:
- fields: float32 [5, 4, 128, 1024], P(None, None, 'lat', 'lon'), may hold values from -6 to 6
- depth: int32 [128], P('lat'), may hold values from 0 to 96, as said below
- frac: float32 [4, 128, 1024], P(None, 'lat', 'lon'), may hold values from 0 to 1
- helm: float32 [4, 128, 1024], P(None, 'lat', 'lon'), may hold values from 0.1 to 2
Outputs:
- departed: float32 [5, 4, 128, 1024], P(None, None, 'lat', 'lon')
- pressure: float32 [4, 128, 1024], P(None, 'lat', 'lon')
Inputs may be any that keep to these rules, and one draw needn't show every extreme that they name: All rows of an aligned band of 8 latitude rows share one depth. A band's depth is either 96 (a jet band) or at most 32, and may be 0. Among the 32 rows of one device (aligned blocks) at most 1 band is a jet band, and in every draw some block has exactly 1.
All inputs are finite; a program needn't handle non-finite values.
Results may differ from a plain program's by a relative error of at most 0.0003.
Values sent between devices are 32-bit elements; how exact they have to be, the bound alone decides.
A program may use at most 128 MiB of HBM per device.

v0:
```python
import functools

import jax
import jax.numpy as jnp
from jax import lax
from jax.experimental import pallas as pl
from jax.experimental.pallas import tpu as pltpu
from jax.sharding import PartitionSpec as P

BAND = 8
SHALLOW = 32
LANES = 128
NEAR = SHALLOW + 4
F32 = jnp.float32
MESH = pl.DeviceIdType.MESH
HALO_FIELDS = (0, 1, 3)
SPARE = 108


def turn(x, shift):
    shift %= LANES
    return x if shift == 0 else pltpu.roll(x, shift, axis=1)


def lane_of(shape):
    return lax.broadcasted_iota(jnp.int32, shape, len(shape) - 1)


def jet_band(depth_ref, bands):
    jet = jnp.int32(0)
    for b in range(1, bands):
        jet = jnp.where(depth_ref[b * BAND] > SHALLOW, b, jet)
    return jet


def interp_weights(frac):
    s = -frac
    below, above = (s - 1.0) * s, (s + 1.0) * (s + 2.0)
    return [
        s * above * (1.0 / 6.0),
        (s - 1.0) * above * -0.5,
        below * (s + 2.0) * 0.5,
        below * (s + 1.0) * (-1.0 / 6.0),
    ]


def depart(own, left, right, depth, weights):
    lane = lane_of(own[0].shape)
    totals = [jnp.zeros_like(own[0]) for _ in own]
    for o, w in zip((-1, 0, 1, 2), weights):
        s = depth + o
        t = lane + s
        shift = (s + LANES) & (LANES - 1)
        for n in range(len(own)):
            x = jnp.where(t <= LANES - 1, own[n], left[n])
            if o == -1:
                x = jnp.where(t == -1, right[n], x)
            totals[n] = totals[n] + w * pltpu.roll(x, shift, axis=1)
    return totals


def depart_beside(own, left, right, depth, weights):
    lane = lane_of(own[0].shape)
    totals = [jnp.zeros_like(own[0]) for _ in own]
    for o, w in zip((-1, 0, 1, 2), weights):
        s = depth + o
        t = lane + s
        shift = (s + LANES) & (LANES - 1)
        for n in range(len(own)):
            x = jnp.where(t <= LANES - 1, left[n], own[n])
            if o < 2:
                x = jnp.where((t >= 0) & (t <= 1), right[n], x)
            if o == -1:
                x = jnp.where(t == -1, own[n], x)
            totals[n] = totals[n] + w * pltpu.roll(x, shift, axis=1)
    return totals


def beside_pair(own, halo):
    lane = lane_of(own.shape)
    first, last = lane == 0, lane == LANES - 1
    return (
        (turn(jnp.where(first, halo, own), -1), turn(jnp.where(last, halo, own), 1)),
        (turn(jnp.where(first, own, halo), -1), turn(jnp.where(last, own, halo), 1)),
    )


ORDER = (0, 1, 3, 2, 4)


def whole_step(lev, clat, depth_hbm, fields_hbm, frac_hbm, helm_hbm, departed, pressure,
               depth_ref, fields, frac, helm, main, edge, top, bottom, dtop, dbottom, gtop, gbottom,
               main_i, edge_i, above, below, la, lb, ra, rb,
               ext, hel, rhs_s, p1_s, wts, in_sem, send_sem, recv_sem):
    bands = clat // BAND
    loads = [
        pltpu.make_async_copy(src, dst, in_sem.at[i])
        for i, (src, dst) in enumerate(
            ((depth_hbm, depth_ref), (fields_hbm, fields), (frac_hbm, frac), (helm_hbm, helm)))
    ]
    for load in loads:
        load.start()
    nlon, nlat = lax.axis_size("lon"), lax.axis_size("lat")
    i, j = lax.axis_index("lon"), lax.axis_index("lat")
    east, west = lax.rem(i + 1, nlon), lax.rem(i + nlon - 1, nlon)
    south, north = lax.rem(j + 1, nlat), lax.rem(j + nlat - 1, nlat)
    peers = [{"lon": a, "lat": b} for a, b in (
        (east, j), (west, j), (i, north), (i, south),
        (east, north), (east, south), (west, north), (west, south))]
    barrier = pltpu.get_barrier_semaphore()
    for peer in peers:
        pl.semaphore_signal(barrier, inc=1, device_id=peer, device_id_type=MESH)

    def copy(n, src, dst, peer):
        return pltpu.make_async_remote_copy(
            src_ref=src, dst_ref=dst, send_sem=send_sem.at[n], recv_sem=recv_sem.at[n],
            device_id=peers[peer], device_id_type=MESH)

    mains = {f: copy(7 + f, main.at[f], main_i.at[f], 0) for f in range(5)}
    west_copy = copy(0, edge, edge_i, 1)
    beyond = [
        copy(1, top, below, 2),
        copy(2, bottom, above, 3),
        copy(3, dtop, lb, 4),
        copy(4, dbottom, la, 5),
        copy(5, gtop, rb, 6),
        copy(6, gbottom, ra, 7),
    ]
    for load in loads:
        load.wait()
    jet = jet_band(depth_ref, bands)
    nk = lev * BAND
    lane = lane_of((nk, LANES))
    jets = jnp.full((nk, LANES), jet)
    rest = None
    for b in range(bands):
        at = SPARE + 3 * b
        rows = pl.ds(b * BAND, BAND)
        fr = turn(frac[:, rows, :].reshape(nk, LANES), at - (LANES - 2))
        he = turn(helm[:, rows, :].reshape(nk, LANES), at + 2 - (LANES - 1))
        rest = fr if rest is None else jnp.where(lane >= at, fr, rest)
        rest = jnp.where(lane >= at + 2, he, rest)
    for f in ORDER:
        x = [fields[f, :, pl.ds(b * BAND, BAND), :].reshape(nk, LANES) for b in range(bands)]
        deep = x[0]
        for b in range(1, bands):
            deep = jnp.where(jets == b, x[b], deep)
        packed = None
        for slot in range(bands - 1):
            y = jnp.where(jets > slot, x[slot], x[slot + 1])
            y = turn(y, slot * NEAR + NEAR - LANES)
            packed = y if packed is None else jnp.where(lane >= slot * NEAR, y, packed)
        if f == 0:
            packed = jnp.where(lane >= SPARE, rest, packed)
        main[f, 0] = deep.reshape(lev, BAND, LANES)
        main[f, 1] = packed.reshape(lev, BAND, LANES)
        if f == ORDER[0]:
            pl.semaphore_wait(barrier, len(peers))
        if f == ORDER[3]:
            acc = jnp.zeros((nk, LANES), F32)
            for b in range(bands):
                rows = pl.ds(b * BAND, BAND)
                for n in range(7):
                    src = fields[n, :, rows, :] if n < 5 else (frac if n == 5 else helm)[:, rows, :]
                    at = 32 * b + (17 if n == 6 else 3 * n)
                    wide = 3 if n < 5 else 7 - n
                    acc = jnp.where((lane >= at) & (lane < at + wide), turn(src.reshape(nk, LANES), at), acc)
            edge[...] = acc.reshape(lev, BAND, LANES)
            west_copy.start()
            lane8 = lane_of((2 * lev, LANES))
            for row, mine, diag, thin, n, at_depth in (
                    (0, top, dtop, gtop, 0, 0), (clat - 2, bottom, dbottom, gbottom, 1, clat - 1)):
                for q in range(5):
                    src = fields.at[HALO_FIELDS[q]] if q < 3 else (frac if q == 3 else helm)
                    for k in range(lev):
                        mine[q, 2 * k:2 * k + 2, :] = src[k, row:row + 2, :]
                mine[5] = jnp.full((2 * lev, LANES), depth_ref[at_depth].astype(F32))
                beyond[n].start()
                u = jnp.where(lane8 < 2, turn(mine[3], 2), mine[0])
                diag[0] = jnp.where(lane8 == 2, turn(mine[4], 3), u)
                diag[1] = mine[1]
                diag[2] = mine[2]
                beyond[2 + n].start()
                g = mine[0]
                for q in range(1, 5):
                    at = 11 if q == 4 else 3 * q
                    g = jnp.where(lane8 >= at, turn(mine[q], at), g)
                thin[...] = g
                beyond[4 + n].start()
        mains[f].start()

    for k in range(lev):
        for o, w in enumerate(interp_weights(frac[k])):
            wts[o, k] = w
        hel[0, k, pl.ds(BAND, clat), :] = helm[k]
    inside = (j > 0, j < nlat - 1)
    flat = lambda x: x.reshape(nk, LANES)
    tall3 = lambda x: x.reshape(lev, BAND, LANES)
    west_copy.wait_recv()
    for f in ORDER:
        mains[f].wait_recv()
        for b in range(bands):
            rows = pl.ds(b * BAND, BAND)
            depth = depth_ref[b * BAND]
            slot = b - (b > jet).astype(jnp.int32)
            amount = (2 * LANES - NEAR - NEAR * slot) & (LANES - 1)
            own = flat(fields[f, :, rows, :])
            left = jnp.where(jets == b, flat(main_i[f, 0]), pltpu.roll(flat(main_i[f, 1]), amount, axis=1))
            brim = flat(edge_i[...])
            right = turn(brim, -(32 * b + 3 * f))
            [got] = depart([own], [left], [right], depth, [flat(wts[o, :, rows, :]) for o in range(4)])
            departed[f, :, rows, :] = tall3(got)
            if f in HALO_FIELDS:
                q = HALO_FIELDS.index(f)
                rest = flat(main_i[0, 1])
                fr = jnp.where(lane < 64, turn(brim, -(32 * b + 15)), turn(rest, 18 - 3 * b))
                [past] = depart_beside([own], [left], [right], depth, interp_weights(fr))
                at = pl.ds((b + 1) * BAND, BAND)
                ext[q, 0, :, at, :] = tall3(got)
                ext[q, 1, :, at, :] = tall3(past)
                if f == 0:
                    he = jnp.where(lane < 64, turn(brim, -(32 * b + 17)), turn(rest, 17 - 3 * b))
                    hel[1, :, at, :] = tall3(he)
        if f == ORDER[2]:
            for c in beyond:
                c.wait_recv()
            solve(lev, clat, inside, helm, above, below, la, lb, ra, rb, ext, hel, rhs_s, p1_s, pressure)
    for c in (west_copy, *beyond, *mains.values()):
        c.wait_send()


def solve(lev, clat, inside, helm, above, below, la, lb, ra, rb, ext, hel, rhs_s, p1_s, pressure):
    lane = lane_of((BAND, LANES))
    for side, (mine, diag, thin) in enumerate(((above, la, ra), (below, lb, rb))):
        depth = jnp.max(mine[5]).astype(jnp.int32)
        own = [mine[q] for q in range(3)]
        left = [diag[q] for q in range(3)]
        g = thin[...]
        right = [turn(g, -3 * q) for q in range(3)]
        fr = jnp.where(lane < 64, turn(g, -9), turn(left[0], -2))
        he = jnp.where(lane < 64, turn(g, -11), turn(left[0], -3))
        got = depart(own, left, right, depth, interp_weights(mine[3]))
        past = depart_beside(own, left, right, depth, interp_weights(fr))
        at = BAND - 2 if side == 0 else BAND + clat
        for k in range(lev):
            pair = slice(2 * k, 2 * k + 2)
            for q in range(3):
                ext[q, 0, k, at:at + 2, :] = jnp.where(inside[side], got[q], 0.0)[pair]
                ext[q, 1, k, at:at + 2, :] = jnp.where(inside[side], past[q], 0.0)[pair]
            hel[0, k, at:at + 2, :] = mine[4][pair]
            hel[1, k, at:at + 2, :] = he[pair]
    tall = clat + BAND
    row = lax.broadcasted_iota(jnp.int32, (lev, tall, LANES), 1)
    outside = ((row == 0) & jnp.logical_not(inside[0])) | ((row == clat + 1) & jnp.logical_not(inside[1]))
    first = BAND - 1
    flat = lambda x: x.reshape(-1, LANES)
    mid, up, down = pl.ds(first, tall), pl.ds(first - 1, tall), pl.ds(first + 1, tall)
    u_all = beside_pair(flat(ext[0, 0, :, mid, :]), flat(ext[0, 1, :, mid, :]))
    phi = [flat(ext[2, h, :, mid, :]) for h in range(2)]
    phi_all = beside_pair(*phi)
    for h in range(2):
        div = 0.5 * (u_all[h][0] - u_all[h][1] + flat(ext[1, h, :, down, :]) - flat(ext[1, h, :, up, :]))
        rhs = phi[h] - 0.5 * div
        around = phi_all[h][0] + phi_all[h][1] + flat(ext[2, h, :, down, :]) + flat(ext[2, h, :, up, :])
        p1 = (rhs + around) / (4.0 + flat(hel[h, :, mid, :]))
        p1_s[h] = jnp.where(outside, 0.0, p1.reshape(lev, tall, LANES))
        if h == 0:
            rhs_s[...] = rhs.reshape(lev, tall, LANES)
    mid = pl.ds(1, clat)
    east, west = beside_pair(flat(p1_s[0, :, mid, :]), flat(p1_s[1, :, mid, :]))[0]
    around = east + west + flat(p1_s[0, :, pl.ds(2, clat), :]) + flat(p1_s[0, :, pl.ds(0, clat), :])
    pressure[...] = ((flat(rhs_s[:, mid, :]) + around) / (4.0 + flat(helm[...]))).reshape(lev, clat, LANES)


def store(departed, pressure, departed_o, pressure_o, sem):
    copies = [pltpu.make_async_copy(departed, departed_o, sem.at[0]), pltpu.make_async_copy(pressure, pressure_o, sem.at[1])]
    for c in copies:
        c.start()
    for c in copies:
        c.wait()


def local(fields, depth, frac, helm):
    lev, clat, clon = fields.shape[1:]
    hbm = pl.BlockSpec(memory_space=pltpu.HBM)
    vmem = pl.BlockSpec(memory_space=pltpu.VMEM)
    sent = [(5, 2, lev, BAND, clon), (lev, BAND, clon), (6, 2 * lev, clon), (6, 2 * lev, clon),
            (3, 2 * lev, clon), (3, 2 * lev, clon), (2 * lev, clon), (2 * lev, clon)]
    tall = clat + 2 * BAND
    departed, pressure = pl.pallas_call(
        functools.partial(whole_step, lev, clat),
        out_shape=[pltpu.VMEM(fields.shape, F32), pltpu.VMEM(frac.shape, F32)],
        in_specs=[hbm] * 4,
        out_specs=[vmem, vmem],
        scratch_shapes=[
            pltpu.SMEM(depth.shape, jnp.int32),
            pltpu.VMEM(fields.shape, F32), pltpu.VMEM(frac.shape, F32), pltpu.VMEM(helm.shape, F32),
            *[pltpu.VMEM(t, F32) for t in sent],
            *[pltpu.VMEM(t, F32) for t in sent],
            pltpu.VMEM((3, 2, lev, tall, clon), F32),
            pltpu.VMEM((2, lev, tall, clon), F32),
            pltpu.VMEM((lev, clat + BAND, clon), F32),
            pltpu.VMEM((2, lev, clat + BAND, clon), F32),
            pltpu.VMEM((4, *frac.shape), F32),
            pltpu.SemaphoreType.DMA((4,)),
            pltpu.SemaphoreType.DMA((12,)),
            pltpu.SemaphoreType.DMA((12,)),
        ],
        compiler_params=pltpu.CompilerParams(collective_id=0, has_side_effects=True, vmem_limit_bytes=24 << 20),
        name="step",
    )(*[pltpu.with_memory_space_constraint(x, pltpu.HBM) for x in (depth, fields, frac, helm)])
    return pl.pallas_call(
        store,
        out_shape=[jax.ShapeDtypeStruct(fields.shape, F32), jax.ShapeDtypeStruct(frac.shape, F32)],
        in_specs=[vmem, vmem],
        out_specs=[hbm, hbm],
        scratch_shapes=[pltpu.SemaphoreType.DMA((2,))],
        compiler_params=pltpu.CompilerParams(vmem_limit_bytes=1 << 20),
        name="store",
    )(*[pltpu.with_memory_space_constraint(x, pltpu.VMEM) for x in (departed, pressure)])


def solution(mesh):
    placed = (P(None, None, "lat", "lon"), P("lat"), P(None, "lat", "lon"), P(None, "lat", "lon"))
    return jax.shard_map(
        local,
        mesh=mesh,
        in_specs=placed,
        out_specs=(P(None, None, "lat", "lon"), P(None, "lat", "lon")),
        check_vma=False,
    )
```

profile of v0, /device:TPU:0, one launch (start us, length us, event | category | flops | bytes accessed | tf_op | source)
XLA Modules:
  0.0 14.4 jit_solution(3596357419366949693)
XLA Ops:
  0.6 13.0 %step.1 = (f32[5,4,32,128]{3,2,1,0:T(8,128)S(1)}, f32[4,32,128]{2,1,0:T(8,128)S(1)}) custom-call(s32[32]{0:T(128)} %depth_hbm.1, f32[5,4,32,128]{3,2,1,0:T(8,128)} %fields_hbm.1, f32[4,32,128]{2,1,0:T(8,128)} %frac_hbm.1, f32[4,32,128]{2,1,0:T(8,128)} %helm_hbm.1), custom_call_target="tpu_custom_call" | custom-call | tf_op jit(solution)/shard_map/step/pallas_call | solution.py:290
  13.7 0.8 %store.1 = (f32[5,4,32,128]{3,2,1,0:T(8,128)}, f32[4,32,128]{2,1,0:T(8,128)}) custom-call(f32[5,4,32,128]{3,2,1,0:T(8,128)S(1)} %get-tuple-element.4.departed, f32[4,32,128]{2,1,0:T(8,128)S(1)} %get-tuple-element.5.pressure), custom_call_target="tpu_custom_call" | custom-call | tf_op jit(solution)/shard_map/store/pallas_call | solution.py:312
where the time goes:
time: 14.6 us; the launch traced here: 14.4 us
  Pallas kernels  13.8 us (95%)
  between operations  0.64 us (4%)
    pallas_call x1, Pallas kernels, local(): pl.pallas_call(functools.partial(whole_step, lev, clat), out_shape=[pltpu...  13 us
    pallas_call x1, Pallas kernels, local(): pl.pallas_call(store, out_shape=[jax.ShapeDtypeStruct(fields.shape, F32),...  0.76 us

commit v1 on v0

--- a/solution.py
+++ b/solution.py
@@ -91,25 +91,46 @@
 def whole_step(lev, clat, depth_hbm, fields_hbm, frac_hbm, helm_hbm, departed, pressure,
                depth_ref, fields, frac, helm, main, edge, top, bottom, dtop, dbottom, gtop, gbottom,
                main_i, edge_i, above, below, la, lb, ra, rb,
-               ext, hel, rhs_s, p1_s, wts, in_sem, send_sem, recv_sem):
+               ext, hel, rhs_s, p1_s, wts, in_sem, send_sem, recv_sem, ready_sem):
     bands = clat // BAND
     loads = [
         pltpu.make_async_copy(src, dst, in_sem.at[i])
         for i, (src, dst) in enumerate(
-            ((depth_hbm, depth_ref), (fields_hbm, fields), (frac_hbm, frac), (helm_hbm, helm)))
+            ((depth_hbm, depth_ref), (frac_hbm, frac), (helm_hbm, helm),
+             *[(fields_hbm.at[f], fields.at[f]) for f in ORDER]))
     ]
     for load in loads:
         load.start()
     nlon, nlat = lax.axis_size("lon"), lax.axis_size("lat")
     i, j = lax.axis_index("lon"), lax.axis_index("lat")
     east, west = lax.rem(i + 1, nlon), lax.rem(i + nlon - 1, nlon)
-    south, north = lax.rem(j + 1, nlat), lax.rem(j + nlat - 1, nlat)
+    south, north = j + 1, j - 1
+    upper, lower = j > 0, j < nlat - 1
+    rows_beyond = upper.astype(jnp.int32) + lower.astype(jnp.int32)
     peers = [{"lon": a, "lat": b} for a, b in (
         (east, j), (west, j), (i, north), (i, south),
         (east, north), (east, south), (west, north), (west, south))]
+
+    def greet(semaphore, side, up, down):
+        pl.semaphore_signal(semaphore, inc=1, device_id=peers[side], device_id_type=MESH)
+        for there, peer in ((upper, up), (lower, down)):
+            @pl.when(there)
+            def _():
+                pl.semaphore_signal(semaphore, inc=1, device_id=peers[peer], device_id_type=MESH)
+
+    first, last = i == 0, i == nlon - 1
+    second = i == 1
     barrier = pltpu.get_barrier_semaphore()
-    for peer in peers:
-        pl.semaphore_signal(barrier, inc=1, device_id=peer, device_id_type=MESH)
+    greet(barrier, 0, 4, 5)
+
+    @pl.when(jnp.logical_not(second))
+    def _():
+        greet(barrier, 1, 6, 7)
+
+    for there, peer in ((upper, 2), (lower, 3)):
+        @pl.when(there)
+        def _():
+            pl.semaphore_signal(barrier, inc=1, device_id=peers[peer], device_id_type=MESH)
 
     def copy(n, src, dst, peer):
         return pltpu.make_async_remote_copy(
@@ -126,7 +147,15 @@
         copy(5, gtop, rb, 6),
         copy(6, gbottom, ra, 7),
     ]
-    for load in loads:
+    def westward():
+        west_copy.start()
+        for n in range(2):
+            @pl.when((upper, lower)[n])
+            def _():
+                beyond[n].start()
+                beyond[4 + n].start()
+
+    for load in loads[:4]:
         load.wait()
     jet = jet_band(depth_ref, bands)
     nk = lev * BAND
@@ -154,19 +183,24 @@
             packed = jnp.where(lane >= SPARE, rest, packed)
         main[f, 0] = deep.reshape(lev, BAND, LANES)
         main[f, 1] = packed.reshape(lev, BAND, LANES)
-        if f == ORDER[0]:
-            pl.semaphore_wait(barrier, len(peers))
-        if f == ORDER[3]:
+        if f != ORDER[0]:
+            mains[f].start()
+        else:
+            @pl.when(last)
+            def _():
+                pl.semaphore_wait(barrier, 2 + 3 * rows_beyond)
+                mains[f].start()
+
+            for load in loads[4:]:
+                load.wait()
             acc = jnp.zeros((nk, LANES), F32)
             for b in range(bands):
                 rows = pl.ds(b * BAND, BAND)
                 for n in range(7):
                     src = fields[n, :, rows, :] if n < 5 else (frac if n == 5 else helm)[:, rows, :]
                     at = 32 * b + (17 if n == 6 else 3 * n)
-                    wide = 3 if n < 5 else 7 - n
-                    acc = jnp.where((lane >= at) & (lane < at + wide), turn(src.reshape(nk, LANES), at), acc)
+                    acc = jnp.where(lane >= at, turn(src.reshape(nk, LANES), at), acc)
             edge[...] = acc.reshape(lev, BAND, LANES)
-            west_copy.start()
             lane8 = lane_of((2 * lev, LANES))
             for row, mine, diag, thin, n, at_depth in (
                     (0, top, dtop, gtop, 0, 0), (clat - 2, bottom, dbottom, gbottom, 1, clat - 1)):
@@ -175,25 +209,55 @@
                     for k in range(lev):
                         mine[q, 2 * k:2 * k + 2, :] = src[k, row:row + 2, :]
                 mine[5] = jnp.full((2 * lev, LANES), depth_ref[at_depth].astype(F32))
-                beyond[n].start()
                 u = jnp.where(lane8 < 2, turn(mine[3], 2), mine[0])
                 diag[0] = jnp.where(lane8 == 2, turn(mine[4], 3), u)
                 diag[1] = mine[1]
                 diag[2] = mine[2]
-                beyond[2 + n].start()
                 g = mine[0]
                 for q in range(1, 5):
                     at = 11 if q == 4 else 3 * q
                     g = jnp.where(lane8 >= at, turn(mine[q], at), g)
                 thin[...] = g
-                beyond[4 + n].start()
-        mains[f].start()
+
+                @pl.when(jnp.logical_not((upper, lower)[n]))
+                def _():
+                    for land in ((above, la, ra), (below, lb, rb))[n]:
+                        land[...] = jnp.zeros_like(land)
+            @pl.when(jnp.logical_not(first | last))
+            def _():
+                pl.semaphore_wait(barrier, 2 + 3 * rows_beyond)
+
+            @pl.when(second)
+            def _():
+                greet(ready_sem, 1, 6, 7)
+
+            @pl.when(first)
+            def _():
+                pl.semaphore_wait(ready_sem, 1 + rows_beyond)
+
+            @pl.when(jnp.logical_not(first))
+            def _():
+                westward()
+
+            for n in range(2):
+                @pl.when((upper, lower)[n])
+                def _():
+                    beyond[2 + n].start()
+
+            @pl.when(jnp.logical_not(last))
+            def _():
+                mains[f].start()
+
+    @pl.when(first)
+    def _():
+        pl.semaphore_wait(barrier, 1 + 2 * rows_beyond)
+        westward()
 
     for k in range(lev):
         for o, w in enumerate(interp_weights(frac[k])):
             wts[o, k] = w
         hel[0, k, pl.ds(BAND, clat), :] = helm[k]
-    inside = (j > 0, j < nlat - 1)
+    inside = (upper, lower)
     flat = lambda x: x.reshape(nk, LANES)
     tall3 = lambda x: x.reshape(lev, BAND, LANES)
     west_copy.wait_recv()
@@ -222,10 +286,16 @@
                     he = jnp.where(lane < 64, turn(brim, -(32 * b + 17)), turn(rest, 17 - 3 * b))
                     hel[1, :, at, :] = tall3(he)
         if f == ORDER[2]:
-            for c in beyond:
-                c.wait_recv()
+            for n, c in enumerate(beyond):
+                @pl.when((lower, upper)[n % 2])
+                def _():
+                    c.wait_recv()
             solve(lev, clat, inside, helm, above, below, la, lb, ra, rb, ext, hel, rhs_s, p1_s, pressure)
-    for c in (west_copy, *beyond, *mains.values()):
+    for n, c in enumerate(beyond):
+        @pl.when((upper, lower)[n % 2])
+        def _():
+            c.wait_send()
+    for c in (west_copy, *mains.values()):
         c.wait_send()
 
 
@@ -302,9 +372,10 @@
             pltpu.VMEM((lev, clat + BAND, clon), F32),
             pltpu.VMEM((2, lev, clat + BAND, clon), F32),
             pltpu.VMEM((4, *frac.shape), F32),
-            pltpu.SemaphoreType.DMA((4,)),
+            pltpu.SemaphoreType.DMA((8,)),
             pltpu.SemaphoreType.DMA((12,)),
             pltpu.SemaphoreType.DMA((12,)),
+            pltpu.SemaphoreType.REGULAR,
         ],
         compiler_params=pltpu.CompilerParams(collective_id=0, has_side_effects=True, vmem_limit_bytes=24 << 20),
         name="step",

time: 14.6 us -> 14.4 us (0.986)
  Pallas kernels: 13.8 us -> 13.6 us
    pallas_call x1, Pallas kernels: 13 us -> 12.8 us  [local(): pl.pallas_call(functools.partial(whole_step, lev, clat), out_shape=[pltpu...]
where the time goes in v1:
time: 14.4 us; the launch traced here: 14.2 us
  Pallas kernels  13.6 us (94%)
  between operations  0.64 us (4%)
    pallas_call x1, Pallas kernels, local(): pl.pallas_call(functools.partial(whole_step, lev, clat), out_shape=[pltpu...  12.8 us
    pallas_call x1, Pallas kernels, local(): pl.pallas_call(store, out_shape=[jax.ShapeDtypeStruct(fields.shape, F32),...  0.76 us

profile of v1, /device:TPU:0, one launch (start us, length us, event | category | flops | bytes accessed | tf_op | source)
XLA Modules:
  0.0 14.2 jit_solution(9187427898822698560)
XLA Ops:
  0.6 12.8 %step.1 = (f32[5,4,32,128]{3,2,1,0:T(8,128)S(1)}, f32[4,32,128]{2,1,0:T(8,128)S(1)}) custom-call(s32[32]{0:T(128)} %depth_hbm.1, f32[5,4,32,128]{3,2,1,0:T(8,128)} %fields_hbm.1, f32[4,32,128]{2,1,0:T(8,128)} %frac_hbm.1, f32[4,32,128]{2,1,0:T(8,128)} %helm_hbm.1), custom_call_target="tpu_custom_call" | custom-call | tf_op jit(solution)/shard_map/step/pallas_call | solution.py:360
  13.5 0.8 %store.1 = (f32[5,4,32,128]{3,2,1,0:T(8,128)}, f32[4,32,128]{2,1,0:T(8,128)}) custom-call(f32[5,4,32,128]{3,2,1,0:T(8,128)S(1)} %get-tuple-element.4.departed, f32[4,32,128]{2,1,0:T(8,128)S(1)} %get-tuple-element.5.pressure), custom_call_target="tpu_custom_call" | custom-call | tf_op jit(solution)/shard_map/store/pallas_call | solution.py:383

commit v2 on v1

--- a/solution.py
+++ b/solution.py
@@ -15,6 +15,9 @@
 MESH = pl.DeviceIdType.MESH
 HALO_FIELDS = (0, 1, 3)
 SPARE = 108
+FILL = 28
+PER_TILE = 3
+REST = ((0, 108), (1, 108), (2, 104), (2, 116))
 
 
 def turn(x, shift):
@@ -91,7 +94,7 @@
 def whole_step(lev, clat, depth_hbm, fields_hbm, frac_hbm, helm_hbm, departed, pressure,
                depth_ref, fields, frac, helm, main, edge, top, bottom, dtop, dbottom, gtop, gbottom,
                main_i, edge_i, above, below, la, lb, ra, rb,
-               ext, hel, rhs_s, p1_s, wts, in_sem, send_sem, recv_sem, ready_sem):
+               ext, hel, rhs_s, p1_s, wts, wts2, in_sem, send_sem, recv_sem, ready_sem):
     bands = clat // BAND
     loads = [
         pltpu.make_async_copy(src, dst, in_sem.at[i])
@@ -99,8 +102,8 @@
             ((depth_hbm, depth_ref), (frac_hbm, frac), (helm_hbm, helm),
              *[(fields_hbm.at[f], fields.at[f]) for f in ORDER]))
     ]
-    for load in loads:
-        load.start()
+    for n in (0, 3, 4, 5, 1, 2, 6, 7):
+        loads[n].start()
     nlon, nlat = lax.axis_size("lon"), lax.axis_size("lat")
     i, j = lax.axis_index("lon"), lax.axis_index("lat")
     east, west = lax.rem(i + 1, nlon), lax.rem(i + nlon - 1, nlon)
@@ -155,34 +158,53 @@
                 beyond[n].start()
                 beyond[4 + n].start()
 
-    for load in loads[:4]:
+    for load in (loads[0], loads[3]):
         load.wait()
     jet = jet_band(depth_ref, bands)
     nk = lev * BAND
     lane = lane_of((nk, LANES))
     jets = jnp.full((nk, LANES), jet)
-    rest = None
-    for b in range(bands):
-        at = SPARE + 3 * b
-        rows = pl.ds(b * BAND, BAND)
-        fr = turn(frac[:, rows, :].reshape(nk, LANES), at - (LANES - 2))
-        he = turn(helm[:, rows, :].reshape(nk, LANES), at + 2 - (LANES - 1))
-        rest = fr if rest is None else jnp.where(lane >= at, fr, rest)
-        rest = jnp.where(lane >= at + 2, he, rest)
+    thin_lane = lane_of((BAND, LANES))
+    last_slot = bands - 2
+    pieces = [(slot, k) for k in range(lev) for slot in range(last_slot)]
+    tail = len(pieces) % PER_TILE * NEAR
+
+    def level(x, k):
+        return x[k * BAND:(k + 1) * BAND]
+
     for f in ORDER:
+        if f == ORDER[1]:
+            rest = None
+            for b in range(bands):
+                at = SPARE + 3 * b
+                rows = pl.ds(b * BAND, BAND)
+                fr = turn(frac[:, rows, :].reshape(nk, LANES), at - (LANES - 2))
+                he = turn(helm[:, rows, :].reshape(nk, LANES), at + 2 - (LANES - 1))
+                rest = fr if rest is None else jnp.where(lane >= at, fr, rest)
+                rest = jnp.where(lane >= at + 2, he, rest)
         x = [fields[f, :, pl.ds(b * BAND, BAND), :].reshape(nk, LANES) for b in range(bands)]
         deep = x[0]
         for b in range(1, bands):
             deep = jnp.where(jets == b, x[b], deep)
-        packed = None
-        for slot in range(bands - 1):
-            y = jnp.where(jets > slot, x[slot], x[slot + 1])
-            y = turn(y, slot * NEAR + NEAR - LANES)
-            packed = y if packed is None else jnp.where(lane >= slot * NEAR, y, packed)
-        if f == 0:
-            packed = jnp.where(lane >= SPARE, rest, packed)
-        main[f, 0] = deep.reshape(lev, BAND, LANES)
-        main[f, 1] = packed.reshape(lev, BAND, LANES)
+        slots = [jnp.where(jets > slot, x[slot], x[slot + 1]) for slot in range(bands - 1)]
+        deep = jnp.where(lane < FILL, turn(slots[last_slot], FILL), deep)
+        main[f, 0:lev] = deep.reshape(lev, BAND, LANES)
+        packed = []
+        for n, (slot, k) in enumerate(pieces):
+            at = n % PER_TILE * NEAR
+            y = turn(level(slots[slot], k), at + NEAR - LANES)
+            if at == 0:
+                packed.append(y)
+            else:
+                packed[-1] = jnp.where(thin_lane >= at, y, packed[-1])
+        for k in range(lev):
+            at = tail + (NEAR - FILL) * k
+            packed[-1] = jnp.where(thin_lane >= at, turn(level(slots[last_slot], k), at + NEAR - LANES), packed[-1])
+        if f == ORDER[1]:
+            for k, (tile, at) in enumerate(REST):
+                packed[tile] = jnp.where(thin_lane >= at, turn(level(rest, k), at - SPARE), packed[tile])
+        for n, y in enumerate(packed):
+            main[f, lev + n] = y
         if f != ORDER[0]:
             mains[f].start()
         else:
@@ -191,7 +213,7 @@
                 pl.semaphore_wait(barrier, 2 + 3 * rows_beyond)
                 mains[f].start()
 
-            for load in loads[4:]:
+            for load in (*loads[1:3], *loads[4:]):
                 load.wait()
             acc = jnp.zeros((nk, LANES), F32)
             for b in range(bands):
@@ -261,30 +283,49 @@
     flat = lambda x: x.reshape(nk, LANES)
     tall3 = lambda x: x.reshape(lev, BAND, LANES)
     west_copy.wait_recv()
+    brim = flat(edge_i[...])
+
+    def parts(f):
+        tiles = [main_i[f, n] for n in range(main_i.shape[1])]
+        near = [
+            jnp.concatenate(
+                [turn(tiles[lev + n // PER_TILE], LANES - NEAR - n % PER_TILE * NEAR)
+                 for n in range(slot, len(pieces), last_slot)], axis=0)
+            for slot in range(last_slot)
+        ]
+        near.append(jnp.concatenate(
+            [jnp.where(thin_lane >= LANES - FILL, turn(tiles[k], -FILL),
+                       turn(tiles[-1], LANES - NEAR - tail - (NEAR - FILL) * k)) for k in range(lev)], axis=0))
+        deep = jnp.concatenate(tiles[:lev], axis=0)
+        for b in range(bands):
+            left = near[min(b, last_slot)]
+            if 0 < b <= last_slot:
+                left = jnp.where(jets < b, near[b - 1], left)
+            yield (flat(fields[f, :, pl.ds(b * BAND, BAND), :]), jnp.where(jets == b, deep, left),
+                   turn(brim, -(32 * b + 3 * f)), depth_ref[b * BAND])
+
     for f in ORDER:
         mains[f].wait_recv()
-        for b in range(bands):
+        for b, (own, left, right, depth) in enumerate(parts(f)):
             rows = pl.ds(b * BAND, BAND)
-            depth = depth_ref[b * BAND]
-            slot = b - (b > jet).astype(jnp.int32)
-            amount = (2 * LANES - NEAR - NEAR * slot) & (LANES - 1)
-            own = flat(fields[f, :, rows, :])
-            left = jnp.where(jets == b, flat(main_i[f, 0]), pltpu.roll(flat(main_i[f, 1]), amount, axis=1))
-            brim = flat(edge_i[...])
-            right = turn(brim, -(32 * b + 3 * f))
             [got] = depart([own], [left], [right], depth, [flat(wts[o, :, rows, :]) for o in range(4)])
             departed[f, :, rows, :] = tall3(got)
             if f in HALO_FIELDS:
-                q = HALO_FIELDS.index(f)
-                rest = flat(main_i[0, 1])
+                ext[HALO_FIELDS.index(f), 0, :, pl.ds((b + 1) * BAND, BAND), :] = tall3(got)
+        if f == ORDER[1]:
+            rest = jnp.concatenate([turn(main_i[f, lev + tile], SPARE - at) for tile, at in REST], axis=0)
+            for b in range(bands):
+                rows = pl.ds(b * BAND, BAND)
                 fr = jnp.where(lane < 64, turn(brim, -(32 * b + 15)), turn(rest, 18 - 3 * b))
-                [past] = depart_beside([own], [left], [right], depth, interp_weights(fr))
-                at = pl.ds((b + 1) * BAND, BAND)
-                ext[q, 0, :, at, :] = tall3(got)
-                ext[q, 1, :, at, :] = tall3(past)
-                if f == 0:
-                    he = jnp.where(lane < 64, turn(brim, -(32 * b + 17)), turn(rest, 17 - 3 * b))
-                    hel[1, :, at, :] = tall3(he)
+                he = jnp.where(lane < 64, turn(brim, -(32 * b + 17)), turn(rest, 17 - 3 * b))
+                for o, w in enumerate(interp_weights(fr)):
+                    wts2[o, :, rows, :] = tall3(w)
+                hel[1, :, pl.ds((b + 1) * BAND, BAND), :] = tall3(he)
+        for g in {ORDER[1]: ORDER[:2], ORDER[2]: ORDER[2:3]}.get(f, ()):
+            for b, (own, left, right, depth) in enumerate(parts(g)):
+                rows = pl.ds(b * BAND, BAND)
+                [past] = depart_beside([own], [left], [right], depth, [flat(wts2[o, :, rows, :]) for o in range(4)])
+                ext[HALO_FIELDS.index(g), 1, :, pl.ds((b + 1) * BAND, BAND), :] = tall3(past)
         if f == ORDER[2]:
             for n, c in enumerate(beyond):
                 @pl.when((lower, upper)[n % 2])
@@ -354,7 +395,7 @@
     lev, clat, clon = fields.shape[1:]
     hbm = pl.BlockSpec(memory_space=pltpu.HBM)
     vmem = pl.BlockSpec(memory_space=pltpu.VMEM)
-    sent = [(5, 2, lev, BAND, clon), (lev, BAND, clon), (6, 2 * lev, clon), (6, 2 * lev, clon),
+    sent = [(5, lev + REST[-1][0] + 1, BAND, clon), (lev, BAND, clon), (6, 2 * lev, clon), (6, 2 * lev, clon),
             (3, 2 * lev, clon), (3, 2 * lev, clon), (2 * lev, clon), (2 * lev, clon)]
     tall = clat + 2 * BAND
     departed, pressure = pl.pallas_call(
@@ -371,6 +412,7 @@
             pltpu.VMEM((2, lev, tall, clon), F32),
             pltpu.VMEM((lev, clat + BAND, clon), F32),
             pltpu.VMEM((2, lev, clat + BAND, clon), F32),
+            pltpu.VMEM((4, *frac.shape), F32),
             pltpu.VMEM((4, *frac.shape), F32),
             pltpu.SemaphoreType.DMA((8,)),
             pltpu.SemaphoreType.DMA((12,)),

time: 14.4 us -> 13.9 us (0.965)
  the two profiles are of different devices: /device:TPU:0 before, /device:TPU:1 now
where the time goes in v2:
time: 13.9 us; the launch traced here: 13.8 us
  Pallas kernels  13.1 us (94%)
  between operations  0.64 us (5%)
    pallas_call x1, Pallas kernels, local(): pl.pallas_call(functools.partial(whole_step, lev, clat), out_shape=[pltpu...  12.4 us
    pallas_call x1, Pallas kernels, local(): pl.pallas_call(store, out_shape=[jax.ShapeDtypeStruct(fields.shape, F32),...  0.76 us

profile of v2, /device:TPU:1, one launch (start us, length us, event | category | flops | bytes accessed | tf_op | source)
XLA Modules:
  0.0 13.8 jit_solution(1856740447770794758)
XLA Ops:
  0.6 12.4 %step.1 = (f32[5,4,32,128]{3,2,1,0:T(8,128)S(1)}, f32[4,32,128]{2,1,0:T(8,128)S(1)}) custom-call(s32[32]{0:T(128)} %depth_hbm.1, f32[5,4,32,128]{3,2,1,0:T(8,128)} %fields_hbm.1, f32[4,32,128]{2,1,0:T(8,128)} %frac_hbm.1, f32[4,32,128]{2,1,0:T(8,128)} %helm_hbm.1), custom_call_target="tpu_custom_call" | custom-call | tf_op jit(solution)/shard_map/step/pallas_call | solution.py:401
  13.0 0.8 %store.1 = (f32[5,4,32,128]{3,2,1,0:T(8,128)}, f32[4,32,128]{2,1,0:T(8,128)}) custom-call(f32[5,4,32,128]{3,2,1,0:T(8,128)S(1)} %get-tuple-element.4.departed, f32[4,32,128]{2,1,0:T(8,128)S(1)} %get-tuple-element.5.pressure), custom_call_target="tpu_custom_call" | custom-call | tf_op jit(solution)/shard_map/store/pallas_call | solution.py:425

commit v3 on v2

--- a/solution.py
+++ b/solution.py
@@ -94,7 +94,7 @@
 def whole_step(lev, clat, depth_hbm, fields_hbm, frac_hbm, helm_hbm, departed, pressure,
                depth_ref, fields, frac, helm, main, edge, top, bottom, dtop, dbottom, gtop, gbottom,
                main_i, edge_i, above, below, la, lb, ra, rb,
-               ext, hel, rhs_s, p1_s, wts, wts2, in_sem, send_sem, recv_sem, ready_sem):
+               ext, hel, rhs_s, p1_s, wts, brink, in_sem, send_sem, recv_sem, ready_sem):
     bands = clat // BAND
     loads = [
         pltpu.make_async_copy(src, dst, in_sem.at[i])
@@ -174,6 +174,8 @@
 
     for f in ORDER:
         if f == ORDER[1]:
+            for n in (4, 1, 2):
+                loads[n].wait()
             rest = None
             for b in range(bands):
                 at = SPARE + 3 * b
@@ -182,6 +184,8 @@
                 he = turn(helm[:, rows, :].reshape(nk, LANES), at + 2 - (LANES - 1))
                 rest = fr if rest is None else jnp.where(lane >= at, fr, rest)
                 rest = jnp.where(lane >= at + 2, he, rest)
+        if f == ORDER[2]:
+            loads[5].wait()
         x = [fields[f, :, pl.ds(b * BAND, BAND), :].reshape(nk, LANES) for b in range(bands)]
         deep = x[0]
         for b in range(1, bands):
@@ -205,16 +209,18 @@
                 packed[tile] = jnp.where(thin_lane >= at, turn(level(rest, k), at - SPARE), packed[tile])
         for n, y in enumerate(packed):
             main[f, lev + n] = y
-        if f != ORDER[0]:
+        if f in ORDER[3:]:
             mains[f].start()
         else:
             @pl.when(last)
             def _():
-                pl.semaphore_wait(barrier, 2 + 3 * rows_beyond)
+                if f == ORDER[0]:
+                    pl.semaphore_wait(barrier, 2 + 3 * rows_beyond)
                 mains[f].start()
 
-            for load in (*loads[1:3], *loads[4:]):
-                load.wait()
+        if f == ORDER[2]:
+            for n in (6, 7):
+                loads[n].wait()
             acc = jnp.zeros((nk, LANES), F32)
             for b in range(bands):
                 rows = pl.ds(b * BAND, BAND)
@@ -257,7 +263,7 @@
             def _():
                 pl.semaphore_wait(ready_sem, 1 + rows_beyond)
 
-            @pl.when(jnp.logical_not(first))
+            @pl.when(jnp.logical_not(first | last))
             def _():
                 westward()
 
@@ -268,24 +274,81 @@
 
             @pl.when(jnp.logical_not(last))
             def _():
-                mains[f].start()
+                for g in ORDER[:3]:
+                    mains[g].start()
 
     @pl.when(first)
     def _():
         pl.semaphore_wait(barrier, 1 + 2 * rows_beyond)
+
+    @pl.when(first | last)
+    def _():
         westward()
 
-    for k in range(lev):
-        for o, w in enumerate(interp_weights(frac[k])):
-            wts[o, k] = w
-        hel[0, k, pl.ds(BAND, clat), :] = helm[k]
     inside = (upper, lower)
     flat = lambda x: x.reshape(nk, LANES)
     tall3 = lambda x: x.reshape(lev, BAND, LANES)
-    west_copy.wait_recv()
-    brim = flat(edge_i[...])
-
-    def parts(f):
+    band_rows = [pl.ds(b * BAND, BAND) for b in range(bands)]
+    ext_rows = [pl.ds((b + 1) * BAND, BAND) for b in range(bands)]
+    depths = [depth_ref[b * BAND] for b in range(bands)]
+    taps = (-1, 0, 1, 2)
+
+    def tap_sum(x, depth, weights):
+        total = None
+        for o, w in zip(taps, weights):
+            term = w * pltpu.roll(x, (depth + o + LANES) & (LANES - 1), axis=1)
+            total = term if total is None else total + term
+        return total
+
+    for b in range(bands):
+        weights = interp_weights(flat(frac[:, band_rows[b], :]))
+        for o, w in zip(taps, weights):
+            wts[o + 1, :, band_rows[b], :] = tall3(jnp.where(lane < depths[b] + o, w, 0.0))
+        brink[:, band_rows[b], :] = tall3(jnp.where((lane == LANES - 1) & (depths[b] == 0), weights[0], 0.0))
+        weights = [jnp.where(lane < depths[b] + o, 0.0, w) for o, w in zip(taps, weights)]
+        weights[0] = jnp.where(lane < LANES - 1 + depths[b], weights[0], 0.0)
+        for f in range(5):
+            departed[f, :, band_rows[b], :] = tall3(tap_sum(flat(fields[f, :, band_rows[b], :]), depths[b], weights))
+        hel[0, :, ext_rows[b], :] = helm[:, band_rows[b], :]
+
+    past_edge = lane >= LANES - 2
+
+    def east_side():
+        west_copy.wait_recv()
+        brim = flat(edge_i[...])
+        for b in range(bands):
+            shore = flat(brink[:, band_rows[b], :])
+            weights = interp_weights(turn(brim, -(32 * b + 15)))
+            got = [flat(departed[f, :, band_rows[b], :]) + shore * turn(brim, -(32 * b + 3 * f + 1)) for f in range(5)]
+            old = [flat(ext[q, 1, :, ext_rows[b], :]) for q in range(3)]
+            he = jnp.where(past_edge, flat(hel[1, :, ext_rows[b], :]), turn(brim, -(32 * b + 17)))
+            past = [
+                tap_sum(jnp.where(lane < 3, turn(brim, -(32 * b + 3 * f)), flat(fields[f, :, band_rows[b], :])), depths[b], weights)
+                for f in HALO_FIELDS
+            ]
+            for f in range(5):
+                departed[f, :, band_rows[b], :] = tall3(got[f])
+            for q, f in enumerate(HALO_FIELDS):
+                ext[q, 0, :, ext_rows[b], :] = tall3(got[f])
+                ext[q, 1, :, ext_rows[b], :] = tall3(jnp.where(past_edge, old[q], past[q]))
+            hel[1, :, ext_rows[b], :] = tall3(he)
+
+    @pl.when(first)
+    def _():
+        east_side()
+
+    mains[ORDER[0]].wait_recv()
+    mains[ORDER[1]].wait_recv()
+    rest = jnp.concatenate([turn(main_i[ORDER[1], lev + tile], SPARE - at) for tile, at in REST], axis=0)
+    for b in range(bands):
+        weights = [jnp.where(past_edge, w, flat(wts[o, :, band_rows[b], :]))
+                   for o, w in enumerate(interp_weights(turn(rest, 18 - 3 * b)))]
+        he = jnp.where(past_edge, turn(rest, 17 - 3 * b), flat(hel[1, :, ext_rows[b], :]))
+        for o in range(4):
+            wts[o, :, band_rows[b], :] = tall3(weights[o])
+        hel[1, :, ext_rows[b], :] = tall3(he)
+
+    def finish(f):
         tiles = [main_i[f, n] for n in range(main_i.shape[1])]
         near = [
             jnp.concatenate(
@@ -297,41 +360,41 @@
             [jnp.where(thin_lane >= LANES - FILL, turn(tiles[k], -FILL),
                        turn(tiles[-1], LANES - NEAR - tail - (NEAR - FILL) * k)) for k in range(lev)], axis=0))
         deep = jnp.concatenate(tiles[:lev], axis=0)
+        old = [flat(departed[f, :, band_rows[b], :]) for b in range(bands)]
+        q = HALO_FIELDS.index(f) if f in HALO_FIELDS else None
+        if q is not None:
+            edge_old = [flat(ext[q, 1, :, ext_rows[b], :]) for b in range(bands)]
+        more = []
         for b in range(bands):
             left = near[min(b, last_slot)]
             if 0 < b <= last_slot:
                 left = jnp.where(jets < b, near[b - 1], left)
-            yield (flat(fields[f, :, pl.ds(b * BAND, BAND), :]), jnp.where(jets == b, deep, left),
-                   turn(brim, -(32 * b + 3 * f)), depth_ref[b * BAND])
+            left = jnp.where(jets == b, deep, left)
+            if q is not None:
+                left = jnp.where((lane == 0) & (depths[b] == 0), flat(fields[f, :, band_rows[b], :]), left)
+            more.append(tap_sum(left, depths[b], [flat(wts[o, :, band_rows[b], :]) for o in range(4)]))
+        for b in range(bands):
+            got = old[b] + jnp.where(past_edge, 0.0, more[b])
+            departed[f, :, band_rows[b], :] = tall3(got)
+            if q is not None:
+                ext[q, 0, :, ext_rows[b], :] = tall3(got)
+                ext[q, 1, :, ext_rows[b], :] = tall3(jnp.where(past_edge, more[b], edge_old[b]))
 
     for f in ORDER:
-        mains[f].wait_recv()
-        for b, (own, left, right, depth) in enumerate(parts(f)):
-            rows = pl.ds(b * BAND, BAND)
-            [got] = depart([own], [left], [right], depth, [flat(wts[o, :, rows, :]) for o in range(4)])
-            departed[f, :, rows, :] = tall3(got)
-            if f in HALO_FIELDS:
-                ext[HALO_FIELDS.index(f), 0, :, pl.ds((b + 1) * BAND, BAND), :] = tall3(got)
-        if f == ORDER[1]:
-            rest = jnp.concatenate([turn(main_i[f, lev + tile], SPARE - at) for tile, at in REST], axis=0)
-            for b in range(bands):
-                rows = pl.ds(b * BAND, BAND)
-                fr = jnp.where(lane < 64, turn(brim, -(32 * b + 15)), turn(rest, 18 - 3 * b))
-                he = jnp.where(lane < 64, turn(brim, -(32 * b + 17)), turn(rest, 17 - 3 * b))
-                for o, w in enumerate(interp_weights(fr)):
-                    wts2[o, :, rows, :] = tall3(w)
-                hel[1, :, pl.ds((b + 1) * BAND, BAND), :] = tall3(he)
-        for g in {ORDER[1]: ORDER[:2], ORDER[2]: ORDER[2:3]}.get(f, ()):
-            for b, (own, left, right, depth) in enumerate(parts(g)):
-                rows = pl.ds(b * BAND, BAND)
-                [past] = depart_beside([own], [left], [right], depth, [flat(wts2[o, :, rows, :]) for o in range(4)])
-                ext[HALO_FIELDS.index(g), 1, :, pl.ds((b + 1) * BAND, BAND), :] = tall3(past)
+        if f not in ORDER[:2]:
+            mains[f].wait_recv()
+        finish(f)
         if f == ORDER[2]:
+            @pl.when(jnp.logical_not(first))
+            def _():
+                east_side()
+
             for n, c in enumerate(beyond):
                 @pl.when((lower, upper)[n % 2])
                 def _():
                     c.wait_recv()
-            solve(lev, clat, inside, helm, above, below, la, lb, ra, rb, ext, hel, rhs_s, p1_s, pressure)
+            halo_rows(lev, clat, inside, above, below, la, lb, ra, rb, ext, hel)
+            solve(lev, clat, inside, helm, ext, hel, rhs_s, p1_s, pressure)
     for n, c in enumerate(beyond):
         @pl.when((upper, lower)[n % 2])
         def _():
@@ -340,8 +403,9 @@
         c.wait_send()
 
 
-def solve(lev, clat, inside, helm, above, below, la, lb, ra, rb, ext, hel, rhs_s, p1_s, pressure):
+def halo_rows(lev, clat, inside, above, below, la, lb, ra, rb, ext, hel):
     lane = lane_of((BAND, LANES))
+    stores = []
     for side, (mine, diag, thin) in enumerate(((above, la, ra), (below, lb, rb))):
         depth = jnp.max(mine[5]).astype(jnp.int32)
         own = [mine[q] for q in range(3)]
@@ -352,14 +416,18 @@
         he = jnp.where(lane < 64, turn(g, -11), turn(left[0], -3))
         got = depart(own, left, right, depth, interp_weights(mine[3]))
         past = depart_beside(own, left, right, depth, interp_weights(fr))
+        for q in range(3):
+            stores.append((side, ext.at[q, 0], jnp.where(inside[side], got[q], 0.0)))
+            stores.append((side, ext.at[q, 1], jnp.where(inside[side], past[q], 0.0)))
+        stores.append((side, hel.at[0], mine[4]))
+        stores.append((side, hel.at[1], he))
+    for side, ref, value in stores:
         at = BAND - 2 if side == 0 else BAND + clat
         for k in range(lev):
-            pair = slice(2 * k, 2 * k + 2)
-            for q in range(3):
-                ext[q, 0, k, at:at + 2, :] = jnp.where(inside[side], got[q], 0.0)[pair]
-                ext[q, 1, k, at:at + 2, :] = jnp.where(inside[side], past[q], 0.0)[pair]
-            hel[0, k, at:at + 2, :] = mine[4][pair]
-            hel[1, k, at:at + 2, :] = he[pair]
+            ref[k, at:at + 2, :] = value[2 * k:2 * k + 2]
+
+
+def solve(lev, clat, inside, helm, ext, hel, rhs_s, p1_s, pressure):
     tall = clat + BAND
     row = lax.broadcasted_iota(jnp.int32, (lev, tall, LANES), 1)
     outside = ((row == 0) & jnp.logical_not(inside[0])) | ((row == clat + 1) & jnp.logical_not(inside[1]))
@@ -369,14 +437,15 @@
     u_all = beside_pair(flat(ext[0, 0, :, mid, :]), flat(ext[0, 1, :, mid, :]))
     phi = [flat(ext[2, h, :, mid, :]) for h in range(2)]
     phi_all = beside_pair(*phi)
+    p1, rhs = [], []
     for h in range(2):
         div = 0.5 * (u_all[h][0] - u_all[h][1] + flat(ext[1, h, :, down, :]) - flat(ext[1, h, :, up, :]))
-        rhs = phi[h] - 0.5 * div
+        rhs.append(phi[h] - 0.5 * div)
         around = phi_all[h][0] + phi_all[h][1] + flat(ext[2, h, :, down, :]) + flat(ext[2, h, :, up, :])
-        p1 = (rhs + around) / (4.0 + flat(hel[h, :, mid, :]))
-        p1_s[h] = jnp.where(outside, 0.0, p1.reshape(lev, tall, LANES))
-        if h == 0:
-            rhs_s[...] = rhs.reshape(lev, tall, LANES)
+        p1.append((rhs[h] + around) / (4.0 + flat(hel[h, :, mid, :])))
+    for h in range(2):
+        p1_s[h] = jnp.where(outside, 0.0, p1[h].reshape(lev, tall, LANES))
+    rhs_s[...] = rhs[0].reshape(lev, tall, LANES)
     mid = pl.ds(1, clat)
     east, west = beside_pair(flat(p1_s[0, :, mid, :]), flat(p1_s[1, :, mid, :]))[0]
     around = east + west + flat(p1_s[0, :, pl.ds(2, clat), :]) + flat(p1_s[0, :, pl.ds(0, clat), :])
@@ -413,7 +482,7 @@
             pltpu.VMEM((lev, clat + BAND, clon), F32),
             pltpu.VMEM((2, lev, clat + BAND, clon), F32),
             pltpu.VMEM((4, *frac.shape), F32),
-            pltpu.VMEM((4, *frac.shape), F32),
+            pltpu.VMEM(frac.shape, F32),
             pltpu.SemaphoreType.DMA((8,)),
             pltpu.SemaphoreType.DMA((12,)),
             pltpu.SemaphoreType.DMA((12,)),

time: 13.9 us -> 13.8 us (level)
  the two profiles are of different devices: /device:TPU:1 before, /device:TPU:0 now
where the time goes in v3:
time: 13.8 us; the launch traced here: 13.6 us
  Pallas kernels  13 us (94%)
  between operations  0.64 us (5%)
    pallas_call x1, Pallas kernels, local(): pl.pallas_call(functools.partial(whole_step, lev, clat), out_shape=[pltpu...  12.2 us
    pallas_call x1, Pallas kernels, local(): pl.pallas_call(store, out_shape=[jax.ShapeDtypeStruct(fields.shape, F32),...  0.76 us

profile of v3, /device:TPU:0, one launch (start us, length us, event | category | flops | bytes accessed | tf_op | source)
XLA Modules:
  0.0 13.6 jit_solution(5796190555699235497)
XLA Ops:
  0.6 12.2 %step.1 = (f32[5,4,32,128]{3,2,1,0:T(8,128)S(1)}, f32[4,32,128]{2,1,0:T(8,128)S(1)}) custom-call(s32[32]{0:T(128)} %depth_hbm.1, f32[5,4,32,128]{3,2,1,0:T(8,128)} %fields_hbm.1, f32[4,32,128]{2,1,0:T(8,128)} %frac_hbm.1, f32[4,32,128]{2,1,0:T(8,128)} %helm_hbm.1), custom_call_target="tpu_custom_call" | custom-call | tf_op jit(solution)/shard_map/step/pallas_call | solution.py:470
  12.9 0.8 %store.1 = (f32[5,4,32,128]{3,2,1,0:T(8,128)}, f32[4,32,128]{2,1,0:T(8,128)}) custom-call(f32[5,4,32,128]{3,2,1,0:T(8,128)S(1)} %get-tuple-element.4.departed, f32[4,32,128]{2,1,0:T(8,128)S(1)} %get-tuple-element.5.pressure), custom_call_target="tpu_custom_call" | custom-call | tf_op jit(solution)/shard_map/store/pallas_call | solution.py:494

commit v4 on v3

--- a/solution.py
+++ b/solution.py
@@ -16,6 +16,7 @@
 HALO_FIELDS = (0, 1, 3)
 SPARE = 108
 FILL = 28
+CHUNK = 25
 PER_TILE = 3
 REST = ((0, 108), (1, 108), (2, 104), (2, 116))
 
@@ -23,6 +24,10 @@
 def turn(x, shift):
     shift %= LANES
     return x if shift == 0 else pltpu.roll(x, shift, axis=1)
+
+
+def turn_rows(x, shift):
+    return pltpu.roll(x, shift % x.shape[0], axis=0)
 
 
 def lane_of(shape):
@@ -123,6 +128,7 @@
 
     first, last = i == 0, i == nlon - 1
     second = i == 1
+    yields = last & (lax.rem(j, 2) == 1)
     barrier = pltpu.get_barrier_semaphore()
     greet(barrier, 0, 4, 5)
 
@@ -210,7 +216,9 @@
         for n, y in enumerate(packed):
             main[f, lev + n] = y
         if f in ORDER[3:]:
-            mains[f].start()
+            @pl.when(jnp.logical_not(yields))
+            def _():
+                mains[f].start()
         else:
             @pl.when(last)
             def _():
@@ -230,21 +238,30 @@
                     acc = jnp.where(lane >= at, turn(src.reshape(nk, LANES), at), acc)
             edge[...] = acc.reshape(lev, BAND, LANES)
             lane8 = lane_of((2 * lev, LANES))
+            row8 = lax.broadcasted_iota(jnp.int32, (2 * lev, LANES), 0)
             for row, mine, diag, thin, n, at_depth in (
                     (0, top, dtop, gtop, 0, 0), (clat - 2, bottom, dbottom, gbottom, 1, clat - 1)):
+                taken = [
+                    [src[k, row:row + 2, :] for k in range(lev)]
+                    for src in (*[fields.at[f] for f in HALO_FIELDS], frac, helm)
+                ]
                 for q in range(5):
-                    src = fields.at[HALO_FIELDS[q]] if q < 3 else (frac if q == 3 else helm)
                     for k in range(lev):
-                        mine[q, 2 * k:2 * k + 2, :] = src[k, row:row + 2, :]
+                        mine[q, 2 * k:2 * k + 2, :] = taken[q][k]
                 mine[5] = jnp.full((2 * lev, LANES), depth_ref[at_depth].astype(F32))
-                u = jnp.where(lane8 < 2, turn(mine[3], 2), mine[0])
-                diag[0] = jnp.where(lane8 == 2, turn(mine[4], 3), u)
-                diag[1] = mine[1]
-                diag[2] = mine[2]
-                g = mine[0]
+                whole = [mine[q] for q in range(5)]
+                odd = turn_rows(whole[0], 1)
+                near, far = [
+                    jnp.where(row8 % 2 == n, turn(whole[0], -at), turn(odd, -at - CHUNK)) for at in (FILL, FILL + 2 * CHUNK)
+                ]
+                wind = jnp.where(lane8 < FILL, turn(whole[4], FILL), whole[1])
+                wind = jnp.where(lane8 < FILL - 1, turn(whole[3], FILL - 1), wind)
+                g = whole[0]
                 for q in range(1, 5):
                     at = 11 if q == 4 else 3 * q
-                    g = jnp.where(lane8 >= at, turn(mine[q], at), g)
+                    g = jnp.where(lane8 >= at, turn(whole[q], at), g)
+                diag[0] = jnp.where(lane8 < CHUNK, near, wind)
+                diag[1] = jnp.where(lane8 < CHUNK, far, whole[2])
                 thin[...] = g
 
                 @pl.when(jnp.logical_not((upper, lower)[n]))
@@ -284,6 +301,11 @@
     @pl.when(first | last)
     def _():
         westward()
+
+    @pl.when(yields)
+    def _():
+        for f in ORDER[3:]:
+            mains[f].start()
 
     inside = (upper, lower)
     flat = lambda x: x.reshape(nk, LANES)
@@ -409,11 +431,15 @@
     for side, (mine, diag, thin) in enumerate(((above, la, ra), (below, lb, rb))):
         depth = jnp.max(mine[5]).astype(jnp.int32)
         own = [mine[q] for q in range(3)]
-        left = [diag[q] for q in range(3)]
+        wind, height = diag[0], diag[1]
+        u = jnp.where(lane < FILL + CHUNK, turn(wind, FILL), turn_rows(turn(wind, FILL + CHUNK), -1))
+        u = jnp.where(lane < FILL + 2 * CHUNK, u, turn(height, FILL + 2 * CHUNK))
+        u = jnp.where(lane < FILL + 3 * CHUNK, u, turn_rows(turn(height, FILL + 3 * CHUNK), -1))
+        left = [u, wind, height]
         g = thin[...]
         right = [turn(g, -3 * q) for q in range(3)]
-        fr = jnp.where(lane < 64, turn(g, -9), turn(left[0], -2))
-        he = jnp.where(lane < 64, turn(g, -11), turn(left[0], -3))
+        fr = jnp.where(lane < 64, turn(g, -9), turn(wind, LANES - FILL + 1))
+        he = jnp.where(lane < 64, turn(g, -11), turn(wind, LANES - FILL))
         got = depart(own, left, right, depth, interp_weights(mine[3]))
         past = depart_beside(own, left, right, depth, interp_weights(fr))
         for q in range(3):
@@ -465,7 +491,7 @@
     hbm = pl.BlockSpec(memory_space=pltpu.HBM)
     vmem = pl.BlockSpec(memory_space=pltpu.VMEM)
     sent = [(5, lev + REST[-1][0] + 1, BAND, clon), (lev, BAND, clon), (6, 2 * lev, clon), (6, 2 * lev, clon),
-            (3, 2 * lev, clon), (3, 2 * lev, clon), (2 * lev, clon), (2 * lev, clon)]
+            (2, 2 * lev, clon), (2, 2 * lev, clon), (2 * lev, clon), (2 * lev, clon)]
     tall = clat + 2 * BAND
     departed, pressure = pl.pallas_call(
         functools.partial(whole_step, lev, clat),

time: 13.8 us -> 13.7 us (level)
  no operation moved by 1% of the time
where the time goes in v4:
time: 13.7 us; the launch traced here: 13.5 us
  Pallas kernels  12.9 us (94%)
  between operations  0.64 us (5%)
    pallas_call x1, Pallas kernels, local(): pl.pallas_call(functools.partial(whole_step, lev, clat), out_shape=[pltpu...  12.1 us
    pallas_call x1, Pallas kernels, local(): pl.pallas_call(store, out_shape=[jax.ShapeDtypeStruct(fields.shape, F32),...  0.76 us

profile of v4, /device:TPU:0, one launch (start us, length us, event | category | flops | bytes accessed | tf_op | source)
XLA Modules:
  0.0 13.5 jit_solution(11244642414514483906)
XLA Ops:
  0.6 12.1 %step.1 = (f32[5,4,32,128]{3,2,1,0:T(8,128)S(1)}, f32[4,32,128]{2,1,0:T(8,128)S(1)}) custom-call(s32[32]{0:T(128)} %depth_hbm.1, f32[5,4,32,128]{3,2,1,0:T(8,128)} %fields_hbm.1, f32[4,32,128]{2,1,0:T(8,128)} %frac_hbm.1, f32[4,32,128]{2,1,0:T(8,128)} %helm_hbm.1), custom_call_target="tpu_custom_call" | custom-call | tf_op jit(solution)/shard_map/step/pallas_call | solution.py:496
  12.8 0.8 %store.1 = (f32[5,4,32,128]{3,2,1,0:T(8,128)}, f32[4,32,128]{2,1,0:T(8,128)}) custom-call(f32[5,4,32,128]{3,2,1,0:T(8,128)S(1)} %get-tuple-element.4.departed, f32[4,32,128]{2,1,0:T(8,128)S(1)} %get-tuple-element.5.pressure), custom_call_target="tpu_custom_call" | custom-call | tf_op jit(solution)/shard_map/store/pallas_call | solution.py:520

commit v5 on v4

--- a/solution.py
+++ b/solution.py
@@ -99,7 +99,7 @@
 def whole_step(lev, clat, depth_hbm, fields_hbm, frac_hbm, helm_hbm, departed, pressure,
                depth_ref, fields, frac, helm, main, edge, top, bottom, dtop, dbottom, gtop, gbottom,
                main_i, edge_i, above, below, la, lb, ra, rb,
-               ext, hel, rhs_s, p1_s, wts, brink, in_sem, send_sem, recv_sem, ready_sem):
+               ext, hel, rhs_s, p1_s, wts, wslot, brink, in_sem, send_sem, recv_sem, ready_sem):
     bands = clat // BAND
     loads = [
         pltpu.make_async_copy(src, dst, in_sem.at[i])
@@ -359,6 +359,53 @@
     def _():
         east_side()
 
+    slot_depths = [jnp.where(jet > slot, depths[slot], depths[slot + 1]) for slot in range(bands - 1)]
+    jet_depth = depths[0]
+    for b in range(1, bands):
+        jet_depth = jnp.where(jet == b, depths[b], jet_depth)
+    for o in range(4):
+        by_band = [flat(wts[o, :, band_rows[b], :]) for b in range(bands)]
+        whole = by_band[0]
+        for b in range(1, bands):
+            whole = jnp.where(jets == b, by_band[b], whole)
+        for slot in range(bands - 1):
+            wslot[o, :, band_rows[slot], :] = tall3(jnp.where(jets > slot, by_band[slot], by_band[slot + 1]))
+        wslot[o, :, band_rows[bands - 1], :] = tall3(whole)
+
+    def finish_whole(f):
+        tiles = [main_i[f, n] for n in range(main_i.shape[1])]
+        old = [flat(departed[f, :, band_rows[b], :]) for b in range(bands)]
+
+        def shifted(x, amount):
+            return pltpu.roll(x, (amount + 2 * LANES) & (LANES - 1), axis=1)
+
+        sums = [[] for _ in range(bands)]
+        for k in range(lev):
+            for slot in range(bands):
+                depth = jet_depth if slot == bands - 1 else slot_depths[slot]
+                total = None
+                for n, o in enumerate(taps):
+                    if slot == bands - 1:
+                        x = shifted(tiles[k], depth + o)
+                    elif slot == last_slot:
+                        x = jnp.where(
+                            thin_lane < depth + o - FILL,
+                            shifted(tiles[-1], depth + o + LANES - NEAR - tail - (NEAR - FILL) * k),
+                            shifted(tiles[k], depth + o - FILL))
+                    else:
+                        at = k * last_slot + slot
+                        x = shifted(tiles[lev + at // PER_TILE], depth + o - NEAR - at % PER_TILE * NEAR)
+                    term = wslot[n, k, band_rows[slot], :] * x
+                    total = term if total is None else total + term
+                sums[slot].append(total)
+        sums = [jnp.concatenate(x, axis=0) for x in sums]
+        for b in range(bands):
+            more = sums[min(b, last_slot)]
+            if 0 < b <= last_slot:
+                more = jnp.where(jets < b, sums[b - 1], more)
+            more = jnp.where(jets == b, sums[bands - 1], more)
+            departed[f, :, band_rows[b], :] = tall3(old[b] + more)
+
     mains[ORDER[0]].wait_recv()
     mains[ORDER[1]].wait_recv()
     rest = jnp.concatenate([turn(main_i[ORDER[1], lev + tile], SPARE - at) for tile, at in REST], axis=0)
@@ -405,7 +452,10 @@
     for f in ORDER:
         if f not in ORDER[:2]:
             mains[f].wait_recv()
-        finish(f)
+        if f in HALO_FIELDS:
+            finish(f)
+        else:
+            finish_whole(f)
         if f == ORDER[2]:
             @pl.when(jnp.logical_not(first))
             def _():
@@ -508,6 +558,7 @@
             pltpu.VMEM((lev, clat + BAND, clon), F32),
             pltpu.VMEM((2, lev, clat + BAND, clon), F32),
             pltpu.VMEM((4, *frac.shape), F32),
+            pltpu.VMEM((4, *frac.shape), F32),
             pltpu.VMEM(frac.shape, F32),
             pltpu.SemaphoreType.DMA((8,)),
             pltpu.SemaphoreType.DMA((12,)),

time: 13.7 us -> 13.6 us (level)
  no operation moved by 1% of the time
where the time goes in v5:
time: 13.6 us; the launch traced here: 13.5 us
  Pallas kernels  12.8 us (94%)
  between operations  0.64 us (5%)
    pallas_call x1, Pallas kernels, local(): pl.pallas_call(functools.partial(whole_step, lev, clat), out_shape=[pltpu...  12.1 us
    pallas_call x1, Pallas kernels, local(): pl.pallas_call(store, out_shape=[jax.ShapeDtypeStruct(fields.shape, F32),...  0.76 us

profile of v5, /device:TPU:0, one launch (start us, length us, event | category | flops | bytes accessed | tf_op | source)
XLA Modules:
  0.0 13.5 jit_solution(6618523797936450688)
XLA Ops:
  0.6 12.1 %step.1 = (f32[5,4,32,128]{3,2,1,0:T(8,128)S(1)}, f32[4,32,128]{2,1,0:T(8,128)S(1)}) custom-call(s32[32]{0:T(128)} %depth_hbm.1, f32[5,4,32,128]{3,2,1,0:T(8,128)} %fields_hbm.1, f32[4,32,128]{2,1,0:T(8,128)} %frac_hbm.1, f32[4,32,128]{2,1,0:T(8,128)} %helm_hbm.1), custom_call_target="tpu_custom_call" | custom-call | tf_op jit(solution)/shard_map/step/pallas_call | solution.py:546
  12.7 0.8 %store.1 = (f32[5,4,32,128]{3,2,1,0:T(8,128)}, f32[4,32,128]{2,1,0:T(8,128)}) custom-call(f32[5,4,32,128]{3,2,1,0:T(8,128)S(1)} %get-tuple-element.4.departed, f32[4,32,128]{2,1,0:T(8,128)S(1)} %get-tuple-element.5.pressure), custom_call_target="tpu_custom_call" | custom-call | tf_op jit(solution)/shard_map/store/pallas_call | solution.py:571

commit v6 on v5

--- a/solution.py
+++ b/solution.py
@@ -107,7 +107,7 @@
             ((depth_hbm, depth_ref), (frac_hbm, frac), (helm_hbm, helm),
              *[(fields_hbm.at[f], fields.at[f]) for f in ORDER]))
     ]
-    for n in (0, 3, 4, 5, 1, 2, 6, 7):
+    for n in (3, 0):
         loads[n].start()
     nlon, nlat = lax.axis_size("lon"), lax.axis_size("lat")
     i, j = lax.axis_index("lon"), lax.axis_index("lat")
@@ -140,6 +140,9 @@
         @pl.when(there)
         def _():
             pl.semaphore_signal(barrier, inc=1, device_id=peers[peer], device_id_type=MESH)
+
+    for n in (4, 5, 1, 2, 6, 7):
+        loads[n].start()
 
     def copy(n, src, dst, peer):
         return pltpu.make_async_remote_copy(

time: 13.6 us -> 13.7 us (level)
  no operation moved by 1% of the time
where the time goes in v6:
time: 13.7 us; the launch traced here: 13.5 us
  Pallas kernels  12.8 us (93%)
  between operations  0.64 us (5%)
    pallas_call x1, Pallas kernels, local(): pl.pallas_call(functools.partial(whole_step, lev, clat), out_shape=[pltpu...  12.1 us
    pallas_call x1, Pallas kernels, local(): pl.pallas_call(store, out_shape=[jax.ShapeDtypeStruct(fields.shape, F32),...  0.76 us

profile of v6, /device:TPU:0, one launch (start us, length us, event | category | flops | bytes accessed | tf_op | source)
XLA Modules:
  0.0 13.5 jit_solution(7339731658092725676)
XLA Ops:
  0.6 12.1 %step.1 = (f32[5,4,32,128]{3,2,1,0:T(8,128)S(1)}, f32[4,32,128]{2,1,0:T(8,128)S(1)}) custom-call(s32[32]{0:T(128)} %depth_hbm.1, f32[5,4,32,128]{3,2,1,0:T(8,128)} %fields_hbm.1, f32[4,32,128]{2,1,0:T(8,128)} %frac_hbm.1, f32[4,32,128]{2,1,0:T(8,128)} %helm_hbm.1), custom_call_target="tpu_custom_call" | custom-call | tf_op jit(solution)/shard_map/step/pallas_call | solution.py:549
  12.7 0.8 %store.1 = (f32[5,4,32,128]{3,2,1,0:T(8,128)}, f32[4,32,128]{2,1,0:T(8,128)}) custom-call(f32[5,4,32,128]{3,2,1,0:T(8,128)S(1)} %get-tuple-element.4.departed, f32[4,32,128]{2,1,0:T(8,128)S(1)} %get-tuple-element.5.pressure), custom_call_target="tpu_custom_call" | custom-call | tf_op jit(solution)/shard_map/store/pallas_call | solution.py:574

commit v7 on v6

--- a/solution.py
+++ b/solution.py
@@ -453,6 +453,13 @@
                 ext[q, 1, :, ext_rows[b], :] = tall3(jnp.where(past_edge, more[b], edge_old[b]))
 
     for f in ORDER:
+        if f == ORDER[4]:
+            for n, c in enumerate(beyond):
+                @pl.when((upper, lower)[n % 2])
+                def _():
+                    c.wait_send()
+            for c in (west_copy, *mains.values()):
+                c.wait_send()
         if f not in ORDER[:2]:
             mains[f].wait_recv()
         if f in HALO_FIELDS:
@@ -470,12 +477,6 @@
                     c.wait_recv()
             halo_rows(lev, clat, inside, above, below, la, lb, ra, rb, ext, hel)
             solve(lev, clat, inside, helm, ext, hel, rhs_s, p1_s, pressure)
-    for n, c in enumerate(beyond):
-        @pl.when((upper, lower)[n % 2])
-        def _():
-            c.wait_send()
-    for c in (west_copy, *mains.values()):
-        c.wait_send()
 
 
 def halo_rows(lev, clat, inside, above, below, la, lb, ra, rb, ext, hel):

time: 13.7 us -> 13.6 us (level)
  no operation moved by 1% of the time
where the time goes in v7:
time: 13.6 us; the launch traced here: 13.5 us
  Pallas kernels  12.8 us (94%)
  between operations  0.64 us (5%)
    pallas_call x1, Pallas kernels, local(): pl.pallas_call(functools.partial(whole_step, lev, clat), out_shape=[pltpu...  12.1 us
    pallas_call x1, Pallas kernels, local(): pl.pallas_call(store, out_shape=[jax.ShapeDtypeStruct(fields.shape, F32),...  0.76 us

profile of v7, /device:TPU:0, one launch (start us, length us, event | category | flops | bytes accessed | tf_op | source)
XLA Modules:
  0.0 13.5 jit_solution(12321540507430480023)
XLA Ops:
  0.6 12.1 %step.1 = (f32[5,4,32,128]{3,2,1,0:T(8,128)S(1)}, f32[4,32,128]{2,1,0:T(8,128)S(1)}) custom-call(s32[32]{0:T(128)} %depth_hbm.1, f32[5,4,32,128]{3,2,1,0:T(8,128)} %fields_hbm.1, f32[4,32,128]{2,1,0:T(8,128)} %frac_hbm.1, f32[4,32,128]{2,1,0:T(8,128)} %helm_hbm.1), custom_call_target="tpu_custom_call" | custom-call | tf_op jit(solution)/shard_map/step/pallas_call | solution.py:550
  12.7 0.8 %store.1 = (f32[5,4,32,128]{3,2,1,0:T(8,128)}, f32[4,32,128]{2,1,0:T(8,128)}) custom-call(f32[5,4,32,128]{3,2,1,0:T(8,128)S(1)} %get-tuple-element.4.departed, f32[4,32,128]{2,1,0:T(8,128)S(1)} %get-tuple-element.5.pressure), custom_call_target="tpu_custom_call" | custom-call | tf_op jit(solution)/shard_map/store/pallas_call | solution.py:575
